TPU v7x, 512 devices: a whole 4x4x16 slice. The times are simulated.
512 devices in a mesh: band: 64 (over z, x_lo, core), fft: 8 (over x_hi, y).
Axes of the slice: x: 4 (x_hi: 2, x_lo: 2; x = x_hi * 2 + x_lo), y: 4, z: 16, core: 2. Of those that a mesh axis runs over, the one named last changes fastest.
Arguments:
- orbitals: float32 [128, 120, 14400], P('band', 'fft'), may hold values from -6 to 6
Outputs:
- exchange: float32 [128, 120, 14400], P('band', 'fft')
All inputs are finite; a program needn't handle non-finite values.
Results may differ from a plain program's by a relative error of at most 0.0003.
Values sent between devices are 32-bit elements; how exact they have to be, the bound alone decides.
A program may use at most 64 MiB of HBM per device.

v0:
```python
import math

import jax
import jax.numpy as jnp
from jax import lax
from jax.sharding import PartitionSpec as P

NG = 120


fraction = 0.25
cell_bohr = 37.25
highest = lax.Precision.HIGHEST


def passed_along(value, axis, steps):
    count = lax.axis_size(axis)
    pairs = [(source, (source + steps) % count) for source in range(count)]
    return lax.ppermute(value, axis, pairs)


def lane_count(size):
    return (2 * (size // 2 + 1) + 127) // 128 * 128


def wave_numbers(number, start, size):
    index = start + jnp.arange(number, dtype=jnp.int32)
    return jnp.where(index <= size // 2, index, index - size).astype(jnp.float32)


def angle_table(size):
    places = jnp.arange(size, dtype=jnp.int32)
    product = places[:, None] * places[None, :] % size
    return product.astype(jnp.float32) * (2.0 * math.pi / size)


def lane_frequency(size, lanes):
    lane = jnp.arange(lanes, dtype=jnp.int32)
    frequency = lane % (lanes // 2)
    return (lane, frequency, frequency < size // 2 + 1)


def forward_table(size, lanes):
    lane, frequency, valid = lane_frequency(size, lanes)
    places = jnp.arange(size, dtype=jnp.int32)
    phase = (places[:, None] * frequency[None, :] % size).astype(jnp.float32) * (
        2.0 * math.pi / size
    )
    table = jnp.where(lane[None, :] < lanes // 2, jnp.cos(phase), -jnp.sin(phase))
    return jnp.where(valid[None, :], table, 0.0)


def inverse_table(size, lanes):
    lane, frequency, valid = lane_frequency(size, lanes)
    places = jnp.arange(size, dtype=jnp.int32)
    phase = (frequency[:, None] * places[None, :] % size).astype(jnp.float32) * (
        2.0 * math.pi / size
    )
    single = (frequency == 0) | (2 * frequency == size)
    weight = jnp.where(single, 1.0, 2.0).astype(jnp.float32) * (1.0 / size**3)
    table = jnp.where(
        lane[:, None] < lanes // 2,
        weight[:, None] * jnp.cos(phase),
        -weight[:, None] * jnp.sin(phase),
    )
    return jnp.where(valid[:, None], table, 0.0)


def kernel_slab(size, lanes, number, start):
    step = 2.0 * math.pi / cell_bohr
    first = wave_numbers(size, 0, size)
    second = wave_numbers(number, start, size)
    lane, frequency, valid = lane_frequency(size, lanes)
    third = frequency.astype(jnp.float32)
    square = step**2 * (
        first[:, None, None] ** 2 + second[None, :, None] ** 2 + third[None, None, :] ** 2
    )
    safe = jnp.where(square > 0, square, 1.0)
    values = jnp.where(square > 0, 4.0 * math.pi / safe, 0.0)
    return jnp.where(valid[None, None, :], values, 0.0)


def transform(data, angles, form, inverse):
    half = data.shape[-1] // 2
    cosine = jnp.einsum(form, jnp.cos(angles), data, precision=highest)
    sine = jnp.einsum(form, jnp.sin(angles), data, precision=highest)
    swapped = jnp.concatenate([sine[..., half:], sine[..., :half]], axis=-1)
    signs = jnp.where(jnp.arange(2 * half) < half, 1.0, -1.0).astype(jnp.float32)
    if inverse:
        return cosine - swapped * signs
    return cosine + swapped * signs


def potentials(codensity, kernel, angles, forward_lanes, inverse_lanes):
    spectrum = jnp.einsum("pxyz,zk->pxyk", codensity, forward_lanes, precision=highest)
    spectrum = transform(spectrum, angles, "vy,pxyk->pxvk", False)
    block = lax.all_to_all(spectrum, "fft", split_axis=2, concat_axis=1, tiled=True)
    block = transform(block, angles, "ux,pxyk->puyk", False)
    block = block * kernel[None]
    block = transform(block, angles, "ux,pxyk->puyk", True)
    spectrum = lax.all_to_all(block, "fft", split_axis=1, concat_axis=2, tiled=True)
    spectrum = transform(spectrum, angles, "vy,pxyk->pxvk", True)
    return jnp.einsum("pxyk,kz->pxyz", spectrum, inverse_lanes, precision=highest)


def body(orbitals):
    orbital_count = orbitals.shape[0]
    plane_count = orbitals.shape[1]
    lanes = lane_count(NG)
    distance = lax.axis_size("band") // 4
    visitors = passed_along(orbitals, "band", distance)
    own_grid = orbitals.reshape(orbital_count, plane_count, NG, NG)
    visit_grid = visitors.reshape(orbital_count, plane_count, NG, NG)
    angles = angle_table(NG)
    forward_lanes = forward_table(NG, lanes)
    inverse_lanes = inverse_table(NG, lanes)
    column_count = NG // lax.axis_size("fft")
    kernel = kernel_slab(NG, lanes, column_count, lax.axis_index("fft") * column_count)

    def solve(codensity):
        return potentials(codensity, kernel, angles, forward_lanes, inverse_lanes)

    def one_pair(state, index):
        left = lax.dynamic_index_in_dim(own_grid, index // orbital_count, 0, keepdims=False)
        right = lax.dynamic_index_in_dim(visit_grid, index % orbital_count, 0, keepdims=False)
        return (state, solve((left * right)[None])[0])

    state, fields = lax.scan(
        one_pair, jnp.int32(0), jnp.arange(orbital_count * orbital_count, dtype=jnp.int32)
    )
    fields = fields.reshape(orbital_count, orbital_count, plane_count, NG, NG)
    near = jnp.sum(fields * visit_grid[None], axis=1)
    far = jnp.sum(fields * own_grid[:, None], axis=0)
    returned = passed_along(far.reshape(orbital_count, plane_count, NG * NG), "band", -distance)
    total = near.reshape(orbital_count, plane_count, NG * NG) + returned
    return -fraction * total


def solution(mesh):
    return jax.shard_map(
        body,
        mesh=mesh,
        in_specs=(P("band", "fft", None),),
        out_specs=P("band", "fft", None),
        check_vma=False,
    )
```

profile of v0, /device:TPU:101, one launch (start us, length us, event | category | flops | bytes accessed | tf_op | source)
XLA Modules:
  0.0 546.9 jit_solution(8163916650593539860)
XLA Ops:
  0.0 8.8 %collective-permute-start = (f32[2,15,14400]{2,0,1:T(2,128)}, f32[2,15,14400]{2,0,1:T(2,128)}, u32[]{:S(2)}, u32[]{:S(2)}) collective-permute-start(f32[2,15,14400]{2,0,1:T(2,128)} %param.3), channel_id=1, source_target_pairs={{0,128},{8,136},{16,144},{24,152},{32,160},{40,168},{48,176},{56,1... | collective-permute-start | bytes 5184008 | tf_op jit(solution)/shard_map/ppermute | solution.py:19
  8.8 4.6 reshape.340
  13.4 1.6 copy.40
  15.2 144.4 %collective-permute-done = f32[2,15,14400]{2,0,1:T(2,128)} collective-permute-done((f32[2,15,14400]{2,0,1:T(2,128)}, f32[2,15,14400]{2,0,1:T(2,128)}, u32[]{:S(2)}, u32[]{:S(2)}) %collective-permute-start) | collective-permute-done | bytes 1728032 | tf_op jit(solution)/shard_map/ppermute | solution.py:19
  159.6 4.6 reshape.341
  164.1 2.9 copy.41
  167.0 244.0 %while.15 = (s32[]{:T(128)}, f32[4,15,120,120]{3,2,1,0:T(8,128)}, s32[4]{0:T(128)S(1)}, f32[2,15,120,120]{3,2,1,0:T(8,128)S(1)}, f32[2,15,120,120]{3,2,1,0:T(8,1...) while((s32[]{:T(128)}, f32[4,15,120,120]{3,2,1,0:T(8,128)}, ...), condition=%wide.region_1.2_spmd.clone.clone.clone, body=%wide.region_0.1_spmd.clone.clone.clone.sunk | while | flops 3324004864 | bytes 61761452 | solution.py:128
  170.4 3.1 fusion.220
  173.4 1.2 convolution_bitcast_fusion.13
  175.0 1.4 fusion.222
  177.3 18.1 %all_to_all.64 = f32[1,15,120,128]{3,0,1,2:T(1,128)S(1)} all-to-all(f32[1,15,120,128]{3,0,1,2:T(1,128)S(1)} %copy.60), channel_id=1, replica_groups=mesh['band'=64,'fft'=8] {'fft'}, dimensions={2} | all-to-all | bytes 1843200 | tf_op jit(solution)/shard_map/while/body/eval_jaxpr/all_to_all | solution.py:97
  197.8 1.5 fusion.224
  199.3 1.2 convolution_bitcast_fusion.15
  200.9 1.4 fusion.226
  202.2 1.9 copy.63
  204.1 6.2 %all-to-all-start.1 = ((f32[1,120,15,128]{3,0,2,1:T(1,128)}), f32[1,120,15,128]{3,0,2,1:T(1,128)S(1)}, u32[]{:S(2)}, u32[]{:S(2)}) async-start(f32[1,120,15,128]{3,0,2,1:T(1,128)} %copy.63), calls=%async_computation.1 | async-start | bytes 1843200 | tf_op jit(solution)/shard_map/while/body/eval_jaxpr/all_to_all | solution.py:101
  210.3 13.2 %all-to-all-done.1 = f32[1,120,15,128]{3,0,2,1:T(1,128)S(1)} async-done(((f32[1,120,15,128]{3,0,2,1:T(1,128)}), f32[1,120,15,128]{3,0,2,1:T(1,128)S(1)}, u32[]{:S(2)}, u32[]{:S(2)}) %all-to-all-start.1) | async-done | bytes 921632 | tf_op jit(solution)/shard_map/while/body/eval_jaxpr/all_to_all | solution.py:101
  223.7 1.2 convolution_bitcast_fusion.16
  225.3 1.4 fusion.228
  226.7 2.8 fusion.229
  232.8 3.1 fusion.220
  235.9 1.2 convolution_bitcast_fusion.13
  237.4 1.4 fusion.222
  239.8 15.9 %all_to_all.64 = f32[1,15,120,128]{3,0,1,2:T(1,128)S(1)} all-to-all(f32[1,15,120,128]{3,0,1,2:T(1,128)S(1)} %copy.60), channel_id=1, replica_groups=mesh['band'=64,'fft'=8] {'fft'}, dimensions={2} | all-to-all | bytes 1843200 | tf_op jit(solution)/shard_map/while/body/eval_jaxpr/all_to_all | solution.py:97
  256.6 1.2 convolution_bitcast_fusion.14
  258.1 1.5 fusion.224
  259.6 1.2 convolution_bitcast_fusion.15
  261.1 1.4 fusion.226
  262.5 1.9 copy.63
  264.4 6.5 %all-to-all-start.1 = ((f32[1,120,15,128]{3,0,2,1:T(1,128)}), f32[1,120,15,128]{3,0,2,1:T(1,128)S(1)}, u32[]{:S(2)}, u32[]{:S(2)}) async-start(f32[1,120,15,128]{3,0,2,1:T(1,128)} %copy.63), calls=%async_computation.1 | async-start | bytes 1843200 | tf_op jit(solution)/shard_map/while/body/eval_jaxpr/all_to_all | solution.py:101
  270.8 13.2 %all-to-all-done.1 = f32[1,120,15,128]{3,0,2,1:T(1,128)S(1)} async-done(((f32[1,120,15,128]{3,0,2,1:T(1,128)}), f32[1,120,15,128]{3,0,2,1:T(1,128)S(1)}, u32[]{:S(2)}, u32[]{:S(2)}) %all-to-all-start.1) | async-done | bytes 921632 | tf_op jit(solution)/shard_map/while/body/eval_jaxpr/all_to_all | solution.py:101
  284.2 1.2 convolution_bitcast_fusion.16
  285.8 1.4 fusion.228
  287.2 2.8 fusion.229
  293.3 3.1 fusion.220
  297.9 1.4 fusion.222
  300.3 15.9 %all_to_all.64 = f32[1,15,120,128]{3,0,1,2:T(1,128)S(1)} all-to-all(f32[1,15,120,128]{3,0,1,2:T(1,128)S(1)} %copy.60), channel_id=1, replica_groups=mesh['band'=64,'fft'=8] {'fft'}, dimensions={2} | all-to-all | bytes 1843200 | tf_op jit(solution)/shard_map/while/body/eval_jaxpr/all_to_all | solution.py:97
  318.6 1.5 fusion.224
  321.6 1.4 fusion.226
  323.0 1.9 copy.63
  324.9 6.5 %all-to-all-start.1 = ((f32[1,120,15,128]{3,0,2,1:T(1,128)}), f32[1,120,15,128]{3,0,2,1:T(1,128)S(1)}, u32[]{:S(2)}, u32[]{:S(2)}) async-start(f32[1,120,15,128]{3,0,2,1:T(1,128)} %copy.63), calls=%async_computation.1 | async-start | bytes 1843200 | tf_op jit(solution)/shard_map/while/body/eval_jaxpr/all_to_all | solution.py:101
  331.4 13.2 %all-to-all-done.1 = f32[1,120,15,128]{3,0,2,1:T(1,128)S(1)} async-done(((f32[1,120,15,128]{3,0,2,1:T(1,128)}), f32[1,120,15,128]{3,0,2,1:T(1,128)S(1)}, u32[]{:S(2)}, u32[]{:S(2)}) %all-to-all-start.1) | async-done | bytes 921632 | tf_op jit(solution)/shard_map/while/body/eval_jaxpr/all_to_all | solution.py:101
  344.7 1.2 convolution_bitcast_fusion.16
  346.3 1.4 fusion.228
  347.7 2.8 fusion.229
  353.8 3.1 fusion.220
  358.4 1.4 fusion.222
  360.8 15.9 %all_to_all.64 = f32[1,15,120,128]{3,0,1,2:T(1,128)S(1)} all-to-all(f32[1,15,120,128]{3,0,1,2:T(1,128)S(1)} %copy.60), channel_id=1, replica_groups=mesh['band'=64,'fft'=8] {'fft'}, dimensions={2} | all-to-all | bytes 1843200 | tf_op jit(solution)/shard_map/while/body/eval_jaxpr/all_to_all | solution.py:97
  379.1 1.5 fusion.224
  382.1 1.4 fusion.226
  383.5 1.9 copy.63
  385.4 6.5 %all-to-all-start.1 = ((f32[1,120,15,128]{3,0,2,1:T(1,128)}), f32[1,120,15,128]{3,0,2,1:T(1,128)S(1)}, u32[]{:S(2)}, u32[]{:S(2)}) async-start(f32[1,120,15,128]{3,0,2,1:T(1,128)} %copy.63), calls=%async_computation.1 | async-start | bytes 1843200 | tf_op jit(solution)/shard_map/while/body/eval_jaxpr/all_to_all | solution.py:101
  391.9 13.2 %all-to-all-done.1 = f32[1,120,15,128]{3,0,2,1:T(1,128)S(1)} async-done(((f32[1,120,15,128]{3,0,2,1:T(1,128)}), f32[1,120,15,128]{3,0,2,1:T(1,128)S(1)}, u32[]{:S(2)}, u32[]{:S(2)}) %all-to-all-start.1) | async-done | bytes 921632 | tf_op jit(solution)/shard_map/while/body/eval_jaxpr/all_to_all | solution.py:101
  405.3 1.2 convolution_bitcast_fusion.16
  406.8 1.4 fusion.228
  408.2 2.8 fusion.229
  411.0 3.2 multiply_reduce_fusion
  414.2 2.4 reshape.362
  416.6 3.7 copy.47
  420.4 7.2 %collective-permute-start.1 = (f32[2,15,14400]{2,0,1:T(2,128)}, f32[2,15,14400]{2,0,1:T(2,128)}, u32[]{:S(2)}, u32[]{:S(2)}) collective-permute-start(f32[2,15,14400]{2,0,1:T(2,128)} %copy.47), channel_id=1, source_target_pairs={{0,384},{8,392},{16,400},{24,408},{32,416},{40,424},{48,432},{56,4... | collective-permute-start | bytes 5184008 | tf_op jit(solution)/shard_map/ppermute | solution.py:19
  427.6 3.9 multiply_reduce_fusion.1
  431.5 3.9 reshape.361
  435.4 106.9 %collective-permute-done.1 = f32[2,15,14400]{2,0,1:T(2,128)} collective-permute-done((f32[2,15,14400]{2,0,1:T(2,128)}, f32[2,15,14400]{2,0,1:T(2,128)}, u32[]{:S(2)}, u32[]{:S(2)}) %collective-permute-start.1) | collective-permute-done | bytes 1728032 | tf_op jit(solution)/shard_map/ppermute | solution.py:19
  542.3 4.5 fusion.148
  (82 shorter events, 24.3 us)
Async XLA Ops:
  0.0 159.6 %collective-permute-start = (f32[2,15,14400]{2,0,1:T(2,128)}, f32[2,15,14400]{2,0,1:T(2,128)}, u32[]{:S(2)}, u32[]{:S(2)}) collective-permute-start(f32[2,15,14400]{2,0,1:T(2,128)} %param.3), channel_id=1, source_target_pairs={{0,128},{8,136},{16,144},{24,152},{32,160},{40,168},{48,176},{56,1... | collective-permute-start | bytes 5184008 | tf_op jit(solution)/shard_map/ppermute | solution.py:19
  167.0 7.6 %copy-start = (f32[2,15,120,120]{3,2,1,0:T(8,128)}, f32[2,15,120,120]{3,2,1,0:T(8,128)S(1)}, u32[]{:S(2)}) copy-start(f32[2,15,120,120]{3,2,1,0:T(8,128)S(1)} %get-tuple-element.470) | copy-start | bytes 5184004 | tf_op jit(solution)/shard_map/while
  204.1 19.5 %all-to-all-start.1 = ((f32[1,120,15,128]{3,0,2,1:T(1,128)}), f32[1,120,15,128]{3,0,2,1:T(1,128)S(1)}, u32[]{:S(2)}, u32[]{:S(2)}) async-start(f32[1,120,15,128]{3,0,2,1:T(1,128)} %copy.63), calls=%async_computation.1 | async-start | bytes 1843200 | tf_op jit(solution)/shard_map/while/body/eval_jaxpr/all_to_all | solution.py:101
  226.7 2.8 copy-start.1
  229.5 7.6 %copy-start = (f32[2,15,120,120]{3,2,1,0:T(8,128)}, f32[2,15,120,120]{3,2,1,0:T(8,128)S(1)}, u32[]{:S(2)}) copy-start(f32[2,15,120,120]{3,2,1,0:T(8,128)S(1)} %get-tuple-element.470) | copy-start | bytes 5184004 | tf_op jit(solution)/shard_map/while
  264.4 19.7 %all-to-all-start.1 = ((f32[1,120,15,128]{3,0,2,1:T(1,128)}), f32[1,120,15,128]{3,0,2,1:T(1,128)S(1)}, u32[]{:S(2)}, u32[]{:S(2)}) async-start(f32[1,120,15,128]{3,0,2,1:T(1,128)} %copy.63), calls=%async_computation.1 | async-start | bytes 1843200 | tf_op jit(solution)/shard_map/while/body/eval_jaxpr/all_to_all | solution.py:101
  287.2 2.8 copy-start.1
  290.0 7.6 %copy-start = (f32[2,15,120,120]{3,2,1,0:T(8,128)}, f32[2,15,120,120]{3,2,1,0:T(8,128)S(1)}, u32[]{:S(2)}) copy-start(f32[2,15,120,120]{3,2,1,0:T(8,128)S(1)} %get-tuple-element.470) | copy-start | bytes 5184004 | tf_op jit(solution)/shard_map/while
  324.9 19.7 %all-to-all-start.1 = ((f32[1,120,15,128]{3,0,2,1:T(1,128)}), f32[1,120,15,128]{3,0,2,1:T(1,128)S(1)}, u32[]{:S(2)}, u32[]{:S(2)}) async-start(f32[1,120,15,128]{3,0,2,1:T(1,128)} %copy.63), calls=%async_computation.1 | async-start | bytes 1843200 | tf_op jit(solution)/shard_map/while/body/eval_jaxpr/all_to_all | solution.py:101
  347.7 2.8 copy-start.1
  350.5 7.6 %copy-start = (f32[2,15,120,120]{3,2,1,0:T(8,128)}, f32[2,15,120,120]{3,2,1,0:T(8,128)S(1)}, u32[]{:S(2)}) copy-start(f32[2,15,120,120]{3,2,1,0:T(8,128)S(1)} %get-tuple-element.470) | copy-start | bytes 5184004 | tf_op jit(solution)/shard_map/while
  385.4 19.7 %all-to-all-start.1 = ((f32[1,120,15,128]{3,0,2,1:T(1,128)}), f32[1,120,15,128]{3,0,2,1:T(1,128)S(1)}, u32[]{:S(2)}, u32[]{:S(2)}) async-start(f32[1,120,15,128]{3,0,2,1:T(1,128)} %copy.63), calls=%async_computation.1 | async-start | bytes 1843200 | tf_op jit(solution)/shard_map/while/body/eval_jaxpr/all_to_all | solution.py:101
  408.2 2.8 copy-start.1
  416.6 11.0 %copy-start.2 = (f32[2,15,120,120]{3,2,0,1:T(8,128)S(1)}, f32[2,15,120,120]{3,2,0,1:T(8,128)}, u32[]{:S(2)}) copy-start(f32[2,15,120,120]{3,2,0,1:T(8,128)} %reshape.341) | copy-start | bytes 5184004
  420.4 122.0 %collective-permute-start.1 = (f32[2,15,14400]{2,0,1:T(2,128)}, f32[2,15,14400]{2,0,1:T(2,128)}, u32[]{:S(2)}, u32[]{:S(2)}) collective-permute-start(f32[2,15,14400]{2,0,1:T(2,128)} %copy.47), channel_id=1, source_target_pairs={{0,384},{8,392},{16,400},{24,408},{32,416},{40,424},{48,432},{56,4... | collective-permute-start | bytes 5184008 | tf_op jit(solution)/shard_map/ppermute | solution.py:19
where the time goes:
time: 548 us; the launch traced here: 547 us
  waiting for transfers between devices  304 us (55%)
  blocking collectives  65.7 us (12%)
  matrix products  65.6 us (12%)
  local copies, waits for them, and re-layouts  46.8 us (9%)
  starting transfers between devices  41.7 us (8%)
  other arithmetic  11.8 us (2%)
  loops' own time  11.1 us (2%)
    ppermute x2, waiting for transfers between devices, passed_along(): return lax.ppermute(value, axis, pairs)  251 us
    all_to_all x4, blocking collectives, potentials(): lax.all_to_all(spectrum, 'fft', split_axis=2, concat_axis=1, tiled=True)  65.7 us
    all_to_all x4, waiting for transfers between devices, potentials(): lax.all_to_all(block, 'fft', split_axis=1, concat_axis=2, tiled=True)  52.9 us
    all_to_all x4, starting transfers between devices, potentials(): lax.all_to_all(block, 'fft', split_axis=1, concat_axis=2, tiled=True)  25.7 us
    dot_general x16, matrix products, transform(): cosine = jnp.einsum(form, jnp.cos(angles), data, precision=highest)  22.5 us
    dot_general x16, matrix products, transform(): sine = jnp.einsum(form, jnp.sin(angles), data, precision=highest)  19.7 us
    ppermute x2, starting transfers between devices, passed_along(): return lax.ppermute(value, axis, pairs)  16 us
    dot_general x4, matrix products, potentials(): jnp.einsum('pxyz,zk->pxyk', codensity, forward_lanes, precision=highest)  12.2 us
  transfers between devices with their start and end apart: 6, of which 6 were waited for; matrix products, arithmetic and copies ran while one was open for 3% of the time, Pallas kernels for 0%

commit v1 on v0

v1 whole, which is shorter than its diff:
```python
import functools
import math

import jax
import jax.numpy as jnp
import ml_dtypes
import numpy as np
from jax import lax
from jax.experimental import pallas as pl
from jax.experimental.pallas import tpu as pltpu
from jax.sharding import PartitionSpec as P

NG = 120
PLANES = 15
ROWS = 16
HALF = 64
GROUP = 8
COLS = HALF // GROUP
TILES = 113
PACKED = 1696
SPAN = PLANES * COLS
CHUNK = 5
FRACTION = 0.25
CELL_BOHR = 37.25
MESH = pl.DeviceIdType.MESH
f32, bf16 = jnp.float32, jnp.bfloat16


def split_const(table):
    high = table.astype(np.float32).astype(ml_dtypes.bfloat16)
    low = (table - high.astype(np.float64)).astype(np.float32).astype(ml_dtypes.bfloat16)
    return high, low


def on_left(table):
    high, low = split_const(table)
    return np.concatenate([high, high, low], axis=1)


def on_right(table):
    high, low = split_const(table)
    return np.concatenate([high, high, low], axis=0)


def tables():
    n = np.arange(NG)
    phase = (n[:, None] * n[None, :] % NG) * (2.0 * math.pi / NG)
    cos, sin = np.cos(phase), np.sin(phase)
    half = NG // 2 + 1
    first = np.zeros((2 * HALF, 128))
    first[:half, :NG] = cos[:half]
    first[HALF : HALF + half, :NG] = -sin[:half]
    wide_cos, wide_sin = np.zeros((128, 128)), np.zeros((128, 128))
    wide_cos[:NG, :NG], wide_sin[:NG, :NG] = cos, sin
    second = np.block([[wide_cos, -wide_sin], [wide_sin, wide_cos]])
    third = np.block([[cos, sin], [-sin, cos]])
    weight = np.full(half, 2.0)
    weight[[0, -1]] = 1.0
    weight *= -FRACTION / NG**3
    last = np.zeros((NG, 2 * HALF))
    last[:, :half] = cos[:, :half] * weight
    last[:, HALF : HALF + half] = -sin[:, :half] * weight
    return (
        on_left(first),
        on_right(second),
        on_left(third),
        on_left(third.T),
        on_right(second.T),
        on_left(last),
    )


def split(value):
    high = value.astype(bf16)
    return high, (value - high.astype(f32)).astype(bf16)


def left_dot(table, value):
    high, low = split(value)
    return jnp.dot(table, jnp.concatenate([high, low, high], axis=0), preferred_element_type=f32)


def right_dot(value, table):
    high, low = split(value)
    return jnp.dot(jnp.concatenate([high, low, high], axis=1), table, preferred_element_type=f32)


def kernel_body(
    steps,
    bands,
    x_ref,
    first_ref,
    second_ref,
    third_ref,
    third_back_ref,
    second_back_ref,
    last_ref,
    out_ref,
    own_in,
    vis_in,
    own,
    vis,
    near,
    far,
    scale,
    send_a,
    got_a,
    send_b,
    got_b,
    packed,
    back,
    in_send,
    in_recv,
    a_send,
    a_recv,
    b_send,
    b_recv,
    out_send,
    out_recv,
    keep_sem,
    go_sem,
):
    band = lax.axis_index("band")
    me = lax.axis_index("fft")
    core = lax.rem(band, 2)
    up = lax.rem(band + steps, bands)
    down = lax.rem(band + bands - steps, bands)
    mate = band + 1 - 2 * core

    barrier = pltpu.get_barrier_semaphore()
    for other in (up, down, mate):
        pl.semaphore_signal(barrier, 1, device_id=(other, me), device_id_type=MESH)
    for r in range(1, GROUP):
        pl.semaphore_signal(
            barrier, 1, device_id=(band, lax.rem(me + r, GROUP)), device_id_type=MESH
        )
    pl.semaphore_wait(barrier, GROUP + 2)

    def in_copy(kind, o):
        return pltpu.make_async_remote_copy(
            x_ref.at[:, o, :],
            (own_in, vis_in)[kind].at[o],
            in_send.at[kind, o],
            in_recv.at[kind, o],
            device_id=((down, up)[kind], me),
            device_id_type=MESH,
        )

    def out_copy(kind, o):
        return pltpu.make_async_remote_copy(
            packed.at[kind, o],
            back.at[kind, o],
            out_send.at[kind, o],
            out_recv.at[kind, o],
            device_id=((up, down)[kind], me),
            device_id_type=MESH,
        )

    def group_copy(sent, got, send_sem, recv_sem, pair, r):
        other = lax.rem(me + r, GROUP)
        return pltpu.make_async_remote_copy(
            sent.at[pair, :, pl.ds(pl.multiple_of(other * SPAN, 8), SPAN), :],
            got.at[pair, :, pl.ds(pl.multiple_of(me * SPAN, 8), SPAN), :],
            send_sem.at[pair, r],
            recv_sem.at[pair, r],
            device_id=(band, other),
            device_id_type=MESH,
        )

    def keep_copy(sent, got, stage, pair):
        place = pl.ds(pl.multiple_of(me * SPAN, 8), SPAN)
        return pltpu.make_async_copy(
            sent.at[pair, :, place, :], got.at[pair, :, place, :], keep_sem.at[stage, pair]
        )

    forth = (send_a, got_a, a_send, a_recv)
    return_trip = (send_b, got_b, b_send, b_recv)

    def start_group(stage, pair):
        arrays = (forth, return_trip)[stage]
        for r in range(1, GROUP):
            group_copy(*arrays, pair, r).start()
        keep_copy(arrays[0], arrays[1], stage, pair).start()

    def wait_group(stage, pair):
        arrays = (forth, return_trip)[stage]
        for r in range(1, GROUP):
            group_copy(*arrays, pair, r).wait_recv()
        keep_copy(arrays[0], arrays[1], stage, pair).wait()

    def wait_group_sent(stage, pair):
        arrays = (forth, return_trip)[stage]
        for r in range(1, GROUP):
            group_copy(*arrays, pair, r).wait_send()

    lane = lax.broadcasted_iota(jnp.int32, (PLANES, 128), 1)

    def unpack(source, target, o):
        def line(group, r, tile_start):
            if r == 0:
                return source[o, :, pl.ds(tile_start, 128)]
            before = source[o, :, pl.ds(tile_start - 128, 128)]
            if r == 16:
                return pltpu.roll(before, 128, 1)
            here = source[o, :, pl.ds(tile_start, 128)]
            return pltpu.roll(jnp.where(lane >= 128 - 8 * r, before, here), 8 * r, 1)

        def one_group(group, carry):
            for r in range(16):
                start = pl.multiple_of((group * 15 + r) * 128, 128)
                if r < 15:
                    value = line(group, r, start)
                else:
                    before = source[o, :, pl.ds(pl.multiple_of(start - 128, 128), 128)]
                    value = pltpu.roll(before, 120, 1)
                target[o, pl.ds(pl.multiple_of((group * 16 + r) * ROWS, 8), PLANES), :] = value
            return carry

        lax.fori_loop(0, 7, one_group, 0)
        for r in range(8):
            y = 112 + r
            if r < 7:
                value = line(7, r, (7 * 15 + r) * 128)
            else:
                value = jnp.concatenate(
                    [source[o, :, y * NG : (y + 1) * NG], jnp.zeros((PLANES, 8), f32)], axis=1
                )
            target[o, y * ROWS : y * ROWS + PLANES, :] = value

    def pack(source, kind, o):
        packed[kind, o, PACKED - 8 : PACKED, :] = jnp.zeros((8, 128), f32)

        def tile(y, s, following):
            value = source[o, pl.ds(pl.multiple_of(y * ROWS, 8), PLANES), :]
            if s:
                value = pltpu.roll(value, 128 - 8 * s, 1)
            if following is None:
                return value
            after = source[o, pl.ds(pl.multiple_of(following * ROWS, 8), PLANES), :]
            return jnp.where(lane < NG - 8 * s, value, pltpu.roll(after, NG - 8 * s, 1))

        def one_group(group, carry):
            for s in range(15):
                y = group * 16 + s
                packed[kind, o, pl.ds(group * 15 + s, PLANES, stride=TILES), :] = tile(y, s, y + 1)
            return carry

        lax.fori_loop(0, 7, one_group, 0)
        for s in range(8):
            y = 112 + s
            packed[kind, o, pl.ds(105 + s, PLANES, stride=TILES), :] = tile(
                y, s, y + 1 if s < 7 else None
            )

    def plane(ref, o, p):
        return ref[o, pl.ds(p, NG, stride=ROWS), :]

    def forward(pair):
        i, j = pair // 2, pair % 2

        def some_planes(step, carry):
            products = []
            for q in range(CHUNK):
                p = step * CHUNK + q
                product = plane(own, i, p) * plane(vis, j, p)
                products.append(jnp.concatenate([product, jnp.zeros((8, 128), f32)], axis=0))
            lines = left_dot(first_ref[...], jnp.concatenate(products, axis=1))
            lines = jnp.concatenate(
                [
                    jnp.concatenate(
                        [
                            lines[:HALF, q * 128 : (q + 1) * 128],
                            lines[HALF:, q * 128 : (q + 1) * 128],
                        ],
                        axis=1,
                    )
                    for q in range(CHUNK)
                ],
                axis=0,
            )
            spectrum = right_dot(lines, second_ref[...])
            for q in range(CHUNK):
                p = step * CHUNK + q
                for d in range(GROUP):
                    place = pl.ds(pl.multiple_of(d * SPAN + p * COLS, 8), COLS)
                    rows = slice(q * HALF + d * COLS, q * HALF + (d + 1) * COLS)
                    send_a[pair, 0, place, :] = spectrum[rows, :128]
                    send_a[pair, 1, place, :] = spectrum[rows, 128:]
            return carry

        lax.fori_loop(0, PLANES // CHUNK, some_planes, 0)

    def middle(pair):
        def two_columns(step, carry):
            columns = [step * 2, step * 2 + 1]
            data = jnp.concatenate(
                [
                    jnp.concatenate(
                        [
                            got_a[pair, 0, pl.ds(v, NG, stride=COLS), :],
                            got_a[pair, 1, pl.ds(v, NG, stride=COLS), :],
                        ],
                        axis=0,
                    )
                    for v in columns
                ],
                axis=1,
            )
            data = left_dot(third_ref[...], data)
            factor = jnp.concatenate([scale[v] for v in columns], axis=1)
            data = left_dot(
                third_back_ref[...], data * jnp.concatenate([factor, factor], axis=0)
            )
            for n, v in enumerate(columns):
                send_b[pair, 0, pl.ds(v, NG, stride=COLS), :] = data[
                    :NG, n * 128 : (n + 1) * 128
                ]
                send_b[pair, 1, pl.ds(v, NG, stride=COLS), :] = data[
                    NG:, n * 128 : (n + 1) * 128
                ]
            return carry

        lax.fori_loop(0, COLS // 2, two_columns, 0)

    def inverse(pair):
        i, j = pair // 2, pair % 2

        def some_planes(step, carry):
            spectra = []
            for q in range(CHUNK):
                p = step * CHUNK + q
                places = [pl.ds(pl.multiple_of(d * SPAN + p * COLS, 8), COLS) for d in range(GROUP)]
                spectra.append(
                    jnp.concatenate(
                        [
                            jnp.concatenate([got_b[pair, c, place, :] for place in places], axis=0)
                            for c in range(2)
                        ],
                        axis=1,
                    )
                )
            lines = right_dot(jnp.concatenate(spectra, axis=0), second_back_ref[...])
            lines = jnp.concatenate(
                [
                    jnp.concatenate(
                        [
                            lines[q * HALF : (q + 1) * HALF, :128],
                            lines[q * HALF : (q + 1) * HALF, 128:],
                        ],
                        axis=0,
                    )
                    for q in range(CHUNK)
                ],
                axis=1,
            )
            field = left_dot(last_ref[...], lines)
            for q in range(CHUNK):
                p = step * CHUNK + q
                value = field[:, q * 128 : (q + 1) * 128]
                to_near, to_far = plane(vis, j, p) * value, plane(own, i, p) * value
                if j:
                    to_near += plane(near, i, p)
                if i:
                    to_far += plane(far, j, p)
                near[i, pl.ds(p, NG, stride=ROWS), :] = to_near
                far[j, pl.ds(p, NG, stride=ROWS), :] = to_far
            return carry

        lax.fori_loop(0, PLANES // CHUNK, some_planes, 0)

    def fold(index):
        return jnp.where(index <= NG // 2, index, index - NG).astype(f32)

    def prepare_scale():
        step = 2.0 * math.pi / CELL_BOHR
        second = fold(lax.broadcasted_iota(jnp.int32, (NG, 128), 0))
        third = fold(lax.broadcasted_iota(jnp.int32, (NG, 128), 1))
        flat = second * second + third * third

        def column(v, carry):
            first = (me * COLS + v).astype(f32)
            square = step**2 * (flat + first * first)
            safe = jnp.where(square > 0, square, 1.0)
            scale[v] = jnp.where(square > 0, 4.0 * math.pi / safe, 0.0)
            return carry

        lax.fori_loop(0, COLS, column, 0)

    def finish(o):
        def one_tile(t, carry):
            rows = pl.ds(t, PLANES, stride=TILES)
            out_ref[o, :, pl.ds(pl.multiple_of(t * 128, 128), 128)] = (
                back[0, o, rows, :] + back[1, o, rows, :]
            )
            return carry

        lax.fori_loop(0, TILES - 1, one_tile, 0)
        rows = pl.ds(TILES - 1, PLANES, stride=TILES)
        total = back[0, o, rows, :] + back[1, o, rows, :]
        out_ref[o, :, (TILES - 1) * 128 :] = total[:, : NG * NG - (TILES - 1) * 128]

    @pl.when(core == 1)
    def _():
        pl.semaphore_wait(go_sem, 1)

    for o in range(2):
        for kind in range(2):
            in_copy(kind, o).start()
    prepare_scale()

    for kind in range(2):
        in_copy(kind, 0).wait_recv()
    unpack(own_in, own, 0)
    unpack(vis_in, vis, 0)
    forward(0)
    start_group(0, 0)

    for o in range(2):
        for kind in range(2):
            in_copy(kind, o).wait_send()

    @pl.when(core == 0)
    def _():
        pl.semaphore_signal(go_sem, 1, device_id=(mate, me), device_id_type=MESH)

    for kind in range(2):
        in_copy(kind, 1).wait_recv()
    unpack(vis_in, vis, 1)
    forward(1)
    start_group(0, 1)
    wait_group(0, 0)
    middle(0)
    start_group(1, 0)
    unpack(own_in, own, 1)
    forward(2)
    start_group(0, 2)
    wait_group(0, 1)
    middle(1)
    start_group(1, 1)
    wait_group(1, 0)
    inverse(0)
    forward(3)
    start_group(0, 3)
    wait_group(0, 2)
    middle(2)
    start_group(1, 2)
    wait_group(1, 1)
    inverse(1)
    pack(near, 0, 0)
    out_copy(0, 0).start()
    wait_group(0, 3)
    middle(3)
    start_group(1, 3)
    wait_group(1, 2)
    inverse(2)
    pack(far, 1, 0)
    out_copy(1, 0).start()
    wait_group(1, 3)
    inverse(3)
    pack(near, 0, 1)
    out_copy(0, 1).start()
    pack(far, 1, 1)
    out_copy(1, 1).start()

    for stage in range(2):
        for pair in range(4):
            wait_group_sent(stage, pair)
    for o in range(2):
        for kind in range(2):
            out_copy(kind, o).wait_recv()
        finish(o)
    for o in range(2):
        for kind in range(2):
            out_copy(kind, o).wait_send()


def body(orbitals):
    bands = lax.axis_size("band")
    steps = bands // 8
    whole = pl.BlockSpec(memory_space=pltpu.VMEM)
    lines = NG * ROWS
    dma = pltpu.SemaphoreType.DMA
    return pl.pallas_call(
        functools.partial(kernel_body, steps, bands),
        out_shape=jax.ShapeDtypeStruct(orbitals.shape, f32),
        in_specs=[pl.BlockSpec(memory_space=pl.ANY)] + [whole] * 6,
        out_specs=whole,
        scratch_shapes=[
            pltpu.VMEM((2, PLANES, NG * NG), f32),
            pltpu.VMEM((2, PLANES, NG * NG), f32),
            pltpu.VMEM((2, lines, 128), f32),
            pltpu.VMEM((2, lines, 128), f32),
            pltpu.VMEM((2, lines, 128), f32),
            pltpu.VMEM((2, lines, 128), f32),
            pltpu.VMEM((COLS, NG, 128), f32),
            pltpu.VMEM((4, 2, GROUP * SPAN, 128), f32),
            pltpu.VMEM((4, 2, GROUP * SPAN, 128), f32),
            pltpu.VMEM((4, 2, GROUP * SPAN, 128), f32),
            pltpu.VMEM((4, 2, GROUP * SPAN, 128), f32),
            pltpu.VMEM((2, 2, PACKED, 128), f32),
            pltpu.VMEM((2, 2, PACKED, 128), f32),
            dma((2, 2)),
            dma((2, 2)),
            dma((4, GROUP)),
            dma((4, GROUP)),
            dma((4, GROUP)),
            dma((4, GROUP)),
            dma((2, 2)),
            dma((2, 2)),
            dma((2, 4)),
            pltpu.SemaphoreType.REGULAR,
        ],
        compiler_params=pltpu.CompilerParams(
            collective_id=0, has_side_effects=True, vmem_limit_bytes=56 << 20
        ),
    )(orbitals.transpose(1, 0, 2), *(jnp.asarray(t) for t in tables()))


def solution(mesh):
    return jax.shard_map(
        body,
        mesh=mesh,
        in_specs=(P("band", "fft", None),),
        out_specs=P("band", "fft", None),
        check_vma=False,
    )
```

time: 548 us -> 196 us (0.36)
  the two profiles are of different devices: /device:TPU:101 before, /device:TPU:65 now
where the time goes in v1:
time: 196 us
  Pallas kernels  192 us (98%)
  local copies, waits for them, and re-layouts  3.59 us (2%)
    pallas_call x1, Pallas kernels, body(): pl.pallas_call(functools.partial(kernel_body, steps, bands), out_shape=ja...  192 us

profile of v1, /device:TPU:65, one launch (start us, length us, event | category | flops | bytes accessed | tf_op | source)
XLA Modules:
  0.0 196.1 jit_solution(16382792142885567096)
XLA Ops:
  0.0 192.5 %shard_map.73 = f32[2,15,14400]{2,1,0:T(8,128)} custom-call(f32[15,2,14400]{2,1,0:T(2,128)} %bitcast.1, bf16[128,384]{1,0:T(8,128)(2,1)} %constant.12.clone.first_ref, bf16[768,256]{1,0:T(8,128)(2,1)} %constant.13.clone.second_ref, bf16[240,720]{1,0:T(8,128)(2,1)} %constant.14.clone.third_ref, bf16[240,720]{1,0:T(8,128)(2,1)} %constant.15.clone.third_back_ref, ...), custom_call_target="tpu_custom_call" | custom-call | tf_op jit(solution)/shard_map/pallas_call | solution.py:483
  192.5 3.6 %copy.8 = f32[2,15,14400]{2,0,1:T(2,128)} copy(f32[2,15,14400]{2,1,0:T(8,128)} %shard_map.73) | data formatting | bytes 3456000 | tf_op jit(solution)/shard_map/pallas_call | solution.py:483

commit v2 on v1

--- a/solution.py
+++ b/solution.py
@@ -12,12 +12,9 @@
 
 NG = 120
 PLANES = 15
-ROWS = 16
 HALF = 64
 GROUP = 8
 COLS = HALF // GROUP
-TILES = 113
-PACKED = 1696
 SPAN = PLANES * COLS
 CHUNK = 5
 FRACTION = 0.25
@@ -95,7 +92,8 @@
     third_back_ref,
     second_back_ref,
     last_ref,
-    out_ref,
+    near_ref,
+    far_ref,
     own_in,
     vis_in,
     own,
@@ -108,7 +106,6 @@
     send_b,
     got_b,
     packed,
-    back,
     in_send,
     in_recv,
     a_send,
@@ -149,7 +146,7 @@
     def out_copy(kind, o):
         return pltpu.make_async_remote_copy(
             packed.at[kind, o],
-            back.at[kind, o],
+            (near_ref, far_ref)[kind].at[:, o, :],
             out_send.at[kind, o],
             out_recv.at[kind, o],
             device_id=((up, down)[kind], me),
@@ -213,7 +210,7 @@
                 else:
                     before = source[o, :, pl.ds(pl.multiple_of(start - 128, 128), 128)]
                     value = pltpu.roll(before, 120, 1)
-                target[o, pl.ds(pl.multiple_of((group * 16 + r) * ROWS, 8), PLANES), :] = value
+                target[o, pl.ds(group * 16 + r, PLANES, stride=NG), :] = value
             return carry
 
         lax.fori_loop(0, 7, one_group, 0)
@@ -225,35 +222,36 @@
                 value = jnp.concatenate(
                     [source[o, :, y * NG : (y + 1) * NG], jnp.zeros((PLANES, 8), f32)], axis=1
                 )
-            target[o, y * ROWS : y * ROWS + PLANES, :] = value
+            target[o, pl.ds(y, PLANES, stride=NG), :] = value
 
     def pack(source, kind, o):
-        packed[kind, o, PACKED - 8 : PACKED, :] = jnp.zeros((8, 128), f32)
-
         def tile(y, s, following):
-            value = source[o, pl.ds(pl.multiple_of(y * ROWS, 8), PLANES), :]
+            value = source[o, pl.ds(y, PLANES, stride=NG), :]
             if s:
                 value = pltpu.roll(value, 128 - 8 * s, 1)
             if following is None:
                 return value
-            after = source[o, pl.ds(pl.multiple_of(following * ROWS, 8), PLANES), :]
+            after = source[o, pl.ds(following, PLANES, stride=NG), :]
             return jnp.where(lane < NG - 8 * s, value, pltpu.roll(after, NG - 8 * s, 1))
 
         def one_group(group, carry):
             for s in range(15):
                 y = group * 16 + s
-                packed[kind, o, pl.ds(group * 15 + s, PLANES, stride=TILES), :] = tile(y, s, y + 1)
+                place = pl.ds(pl.multiple_of((group * 15 + s) * 128, 128), 128)
+                packed[kind, o, :, place] = tile(y, s, y + 1)
             return carry
 
         lax.fori_loop(0, 7, one_group, 0)
         for s in range(8):
             y = 112 + s
-            packed[kind, o, pl.ds(105 + s, PLANES, stride=TILES), :] = tile(
-                y, s, y + 1 if s < 7 else None
-            )
+            start = (105 + s) * 128
+            if s < 7:
+                packed[kind, o, :, start : start + 128] = tile(y, s, y + 1)
+            else:
+                packed[kind, o, :, start:] = tile(y, s, None)[:, : NG * NG - start]
 
     def plane(ref, o, p):
-        return ref[o, pl.ds(p, NG, stride=ROWS), :]
+        return ref[o, pl.ds(pl.multiple_of(p * NG, 8), NG), :]
 
     def forward(pair):
         i, j = pair // 2, pair % 2
@@ -362,8 +360,8 @@
                     to_near += plane(near, i, p)
                 if i:
                     to_far += plane(far, j, p)
-                near[i, pl.ds(p, NG, stride=ROWS), :] = to_near
-                far[j, pl.ds(p, NG, stride=ROWS), :] = to_far
+                near[i, pl.ds(pl.multiple_of(p * NG, 8), NG), :] = to_near
+                far[j, pl.ds(pl.multiple_of(p * NG, 8), NG), :] = to_far
             return carry
 
         lax.fori_loop(0, PLANES // CHUNK, some_planes, 0)
@@ -386,19 +384,6 @@
 
         lax.fori_loop(0, COLS, column, 0)
 
-    def finish(o):
-        def one_tile(t, carry):
-            rows = pl.ds(t, PLANES, stride=TILES)
-            out_ref[o, :, pl.ds(pl.multiple_of(t * 128, 128), 128)] = (
-                back[0, o, rows, :] + back[1, o, rows, :]
-            )
-            return carry
-
-        lax.fori_loop(0, TILES - 1, one_tile, 0)
-        rows = pl.ds(TILES - 1, PLANES, stride=TILES)
-        total = back[0, o, rows, :] + back[1, o, rows, :]
-        out_ref[o, :, (TILES - 1) * 128 :] = total[:, : NG * NG - (TILES - 1) * 128]
-
     @pl.when(core == 1)
     def _():
         pl.semaphore_wait(go_sem, 1)
@@ -414,6 +399,9 @@
     unpack(vis_in, vis, 0)
     forward(0)
     start_group(0, 0)
+    wait_group(0, 0)
+    middle(0)
+    start_group(1, 0)
 
     for o in range(2):
         for kind in range(2):
@@ -423,34 +411,26 @@
     def _():
         pl.semaphore_signal(go_sem, 1, device_id=(mate, me), device_id_type=MESH)
 
-    for kind in range(2):
-        in_copy(kind, 1).wait_recv()
+    in_copy(1, 1).wait_recv()
     unpack(vis_in, vis, 1)
     forward(1)
     start_group(0, 1)
-    wait_group(0, 0)
-    middle(0)
-    start_group(1, 0)
+    in_copy(0, 1).wait_recv()
     unpack(own_in, own, 1)
     forward(2)
     start_group(0, 2)
-    wait_group(0, 1)
-    middle(1)
-    start_group(1, 1)
+    forward(3)
+    start_group(0, 3)
     wait_group(1, 0)
     inverse(0)
-    forward(3)
-    start_group(0, 3)
-    wait_group(0, 2)
-    middle(2)
-    start_group(1, 2)
+    for pair in range(1, 4):
+        wait_group(0, pair)
+        middle(pair)
+        start_group(1, pair)
     wait_group(1, 1)
     inverse(1)
     pack(near, 0, 0)
     out_copy(0, 0).start()
-    wait_group(0, 3)
-    middle(3)
-    start_group(1, 3)
     wait_group(1, 2)
     inverse(2)
     pack(far, 1, 0)
@@ -468,7 +448,6 @@
     for o in range(2):
         for kind in range(2):
             out_copy(kind, o).wait_recv()
-        finish(o)
     for o in range(2):
         for kind in range(2):
             out_copy(kind, o).wait_send()
@@ -478,13 +457,15 @@
     bands = lax.axis_size("band")
     steps = bands // 8
     whole = pl.BlockSpec(memory_space=pltpu.VMEM)
-    lines = NG * ROWS
+    lines = NG * PLANES
     dma = pltpu.SemaphoreType.DMA
-    return pl.pallas_call(
+    by_plane = orbitals.transpose(1, 0, 2)
+    sums = jax.ShapeDtypeStruct(by_plane.shape, f32)
+    near, far = pl.pallas_call(
         functools.partial(kernel_body, steps, bands),
-        out_shape=jax.ShapeDtypeStruct(orbitals.shape, f32),
+        out_shape=(sums, sums),
         in_specs=[pl.BlockSpec(memory_space=pl.ANY)] + [whole] * 6,
-        out_specs=whole,
+        out_specs=(pl.BlockSpec(memory_space=pl.ANY), pl.BlockSpec(memory_space=pl.ANY)),
         scratch_shapes=[
             pltpu.VMEM((2, PLANES, NG * NG), f32),
             pltpu.VMEM((2, PLANES, NG * NG), f32),
@@ -497,8 +478,7 @@
             pltpu.VMEM((4, 2, GROUP * SPAN, 128), f32),
             pltpu.VMEM((4, 2, GROUP * SPAN, 128), f32),
             pltpu.VMEM((4, 2, GROUP * SPAN, 128), f32),
-            pltpu.VMEM((2, 2, PACKED, 128), f32),
-            pltpu.VMEM((2, 2, PACKED, 128), f32),
+            pltpu.VMEM((2, 2, PLANES, NG * NG), f32),
             dma((2, 2)),
             dma((2, 2)),
             dma((4, GROUP)),
@@ -513,7 +493,8 @@
         compiler_params=pltpu.CompilerParams(
             collective_id=0, has_side_effects=True, vmem_limit_bytes=56 << 20
         ),
-    )(orbitals.transpose(1, 0, 2), *(jnp.asarray(t) for t in tables()))
+    )(by_plane, *(jnp.asarray(t) for t in tables()))
+    return (near + far).transpose(1, 0, 2)
 
 
 def solution(mesh):

time: 196 us -> 189 us (0.964)
  the two profiles are of different devices: /device:TPU:65 before, /device:TPU:49 now
where the time goes in v2:
time: 189 us
  Pallas kernels  185 us (98%)
  other arithmetic  4.08 us (2%)
    pallas_call x1, Pallas kernels, body(): pl.pallas_call(functools.partial(kernel_body, steps, bands), out_shape=(s...  185 us
    transpose x1, other arithmetic, body(): return (near + far).transpose(1, 0, 2)  4.08 us

profile of v2, /device:TPU:49, one launch (start us, length us, event | category | flops | bytes accessed | tf_op | source)
XLA Modules:
  0.0 188.9 jit_solution(12359841703176530459)
XLA Ops:
  0.0 184.8 %shard_map.73 = (f32[15,2,14400]{2,1,0:T(2,128)}, f32[15,2,14400]{2,1,0:T(2,128)}) custom-call(f32[15,2,14400]{2,1,0:T(2,128)} %bitcast.3, bf16[128,384]{1,0:T(8,128)(2,1)} %constant.12.clone.first_ref, bf16[768,256]{1,0:T(8,128)(2,1)} %constant.13.clone.second_ref, bf16[240,720]{1,0:T(8,128)(2,1)} %constant.14.clone.third_ref, ...), custom_call_target="tpu_custom_call" | custom-call | tf_op jit(solution)/shard_map/pallas_call | solution.py:464
  184.8 4.1 %add_bitcast_fusion = f32[2,15,14400]{2,0,1:T(2,128)} fusion(f32[15,2,14400]{2,1,0:T(2,128)} %get-tuple-element.7, f32[15,2,14400]{2,1,0:T(2,128)} %get-tuple-element.8), kind=kLoop, calls=%fused_computation | loop fusion | flops 432000 | bytes 5184000 | tf_op jit(solution)/shard_map/transpose | solution.py:497

commit v3 on v2

--- a/solution.py
+++ b/solution.py
@@ -123,22 +123,28 @@
     up = lax.rem(band + steps, bands)
     down = lax.rem(band + bands - steps, bands)
     mate = band + 1 - 2 * core
+    chip = bands // 16
+    odd = lax.rem(lax.div(band, chip), 2)
+    beside = [
+        lax.rem(first + step + bands, bands) for first in (band, mate) for step in (chip, -chip)
+    ]
 
     barrier = pltpu.get_barrier_semaphore()
-    for other in (up, down, mate):
+    for other in (up, down, *beside):
         pl.semaphore_signal(barrier, 1, device_id=(other, me), device_id_type=MESH)
     for r in range(1, GROUP):
         pl.semaphore_signal(
             barrier, 1, device_id=(band, lax.rem(me + r, GROUP)), device_id_type=MESH
         )
-    pl.semaphore_wait(barrier, GROUP + 2)
-
-    def in_copy(kind, o):
+    pl.semaphore_wait(barrier, GROUP + 5)
+
+    def in_copy(kind, o, part):
+        place = pl.ds(*((0, 11264), (11264, 3136))[part])
         return pltpu.make_async_remote_copy(
-            x_ref.at[:, o, :],
-            (own_in, vis_in)[kind].at[o],
-            in_send.at[kind, o],
-            in_recv.at[kind, o],
+            x_ref.at[:, o, place],
+            (own_in, vis_in)[kind].at[o, :, place],
+            in_send.at[kind, o, part],
+            in_recv.at[kind, o, part],
             device_id=((down, up)[kind], me),
             device_id_type=MESH,
         )
@@ -384,38 +390,52 @@
 
         lax.fori_loop(0, COLS, column, 0)
 
-    @pl.when(core == 1)
+    @pl.when(core + odd > 0)
     def _():
-        pl.semaphore_wait(go_sem, 1)
+        pl.semaphore_wait(go_sem, 2)
 
     for o in range(2):
-        for kind in range(2):
-            in_copy(kind, o).start()
+        for part in range(2):
+            for kind in range(2):
+                in_copy(kind, o, part).start()
     prepare_scale()
 
     for kind in range(2):
-        in_copy(kind, 0).wait_recv()
+        for part in range(2):
+            in_copy(kind, 0, part).wait_recv()
     unpack(own_in, own, 0)
     unpack(vis_in, vis, 0)
     forward(0)
     start_group(0, 0)
+
+    for kind in range(2):
+        for o, part in ((0, 0), (0, 1), (1, 0)):
+            in_copy(kind, o, part).wait_send()
+
+    @pl.when(odd == 0)
+    def _():
+        for other in beside[:2]:
+            pl.semaphore_signal(go_sem, 1, device_id=(other, me), device_id_type=MESH)
+
+    @pl.when((odd == 1) & (core == 0))
+    def _():
+        for other in beside[2:]:
+            pl.semaphore_signal(go_sem, 1, device_id=(other, me), device_id_type=MESH)
+
     wait_group(0, 0)
     middle(0)
     start_group(1, 0)
 
-    for o in range(2):
-        for kind in range(2):
-            in_copy(kind, o).wait_send()
-
-    @pl.when(core == 0)
-    def _():
-        pl.semaphore_signal(go_sem, 1, device_id=(mate, me), device_id_type=MESH)
-
-    in_copy(1, 1).wait_recv()
+    for kind in range(2):
+        in_copy(kind, 1, 1).wait_send()
+
+    for part in range(2):
+        in_copy(1, 1, part).wait_recv()
     unpack(vis_in, vis, 1)
     forward(1)
     start_group(0, 1)
-    in_copy(0, 1).wait_recv()
+    for part in range(2):
+        in_copy(0, 1, part).wait_recv()
     unpack(own_in, own, 1)
     forward(2)
     start_group(0, 2)
@@ -479,8 +499,8 @@
             pltpu.VMEM((4, 2, GROUP * SPAN, 128), f32),
             pltpu.VMEM((4, 2, GROUP * SPAN, 128), f32),
             pltpu.VMEM((2, 2, PLANES, NG * NG), f32),
-            dma((2, 2)),
-            dma((2, 2)),
+            dma((2, 2, 2)),
+            dma((2, 2, 2)),
             dma((4, GROUP)),
             dma((4, GROUP)),
             dma((4, GROUP)),

time: 189 us -> 178 us (0.942)
  the two profiles are of different devices: /device:TPU:49 before, /device:TPU:33 now
where the time goes in v3:
time: 178 us
  Pallas kernels  174 us (98%)
  other arithmetic  4.08 us (2%)
    pallas_call x1, Pallas kernels, body(): pl.pallas_call(functools.partial(kernel_body, steps, bands), out_shape=(s...  174 us
    transpose x1, other arithmetic, body(): return (near + far).transpose(1, 0, 2)  4.08 us

profile of v3, /device:TPU:33, one launch (start us, length us, event | category | flops | bytes accessed | tf_op | source)
XLA Modules:
  0.0 177.8 jit_solution(1254483521911619602)
XLA Ops:
  0.0 173.7 %shard_map.73 = (f32[15,2,14400]{2,1,0:T(2,128)}, f32[15,2,14400]{2,1,0:T(2,128)}) custom-call(f32[15,2,14400]{2,1,0:T(2,128)} %bitcast.3, bf16[128,384]{1,0:T(8,128)(2,1)} %constant.12.clone.first_ref, bf16[768,256]{1,0:T(8,128)(2,1)} %constant.13.clone.second_ref, bf16[240,720]{1,0:T(8,128)(2,1)} %constant.14.clone.third_ref, ...), custom_call_target="tpu_custom_call" | custom-call | tf_op jit(solution)/shard_map/pallas_call | solution.py:484
  173.7 4.1 %add_bitcast_fusion = f32[2,15,14400]{2,0,1:T(2,128)} fusion(f32[15,2,14400]{2,1,0:T(2,128)} %get-tuple-element.7, f32[15,2,14400]{2,1,0:T(2,128)} %get-tuple-element.8), kind=kLoop, calls=%fused_computation | loop fusion | flops 432000 | bytes 5184000 | tf_op jit(solution)/shard_map/transpose | solution.py:517

commit v4 on v3

--- a/solution.py
+++ b/solution.py
@@ -149,12 +149,13 @@
             device_id_type=MESH,
         )
 
-    def out_copy(kind, o):
+    def out_copy(kind, o, part):
+        place = pl.ds(*((0, 7680), (7680, 6720))[part])
         return pltpu.make_async_remote_copy(
-            packed.at[kind, o],
-            (near_ref, far_ref)[kind].at[:, o, :],
-            out_send.at[kind, o],
-            out_recv.at[kind, o],
+            packed.at[kind, o, :, place],
+            (near_ref, far_ref)[kind].at[:, o, place],
+            out_send.at[kind, o, part],
+            out_recv.at[kind, o, part],
             device_id=((up, down)[kind], me),
             device_id_type=MESH,
         )
@@ -230,7 +231,7 @@
                 )
             target[o, pl.ds(y, PLANES, stride=NG), :] = value
 
-    def pack(source, kind, o):
+    def pack(source, kind, o, part):
         def tile(y, s, following):
             value = source[o, pl.ds(y, PLANES, stride=NG), :]
             if s:
@@ -247,8 +248,8 @@
                 packed[kind, o, :, place] = tile(y, s, y + 1)
             return carry
 
-        lax.fori_loop(0, 7, one_group, 0)
-        for s in range(8):
+        lax.fori_loop(4 * part, (4, 7)[part], one_group, 0)
+        for s in range(8 * part):
             y = 112 + s
             start = (105 + s) * 128
             if s < 7:
@@ -449,28 +450,33 @@
         start_group(1, pair)
     wait_group(1, 1)
     inverse(1)
-    pack(near, 0, 0)
-    out_copy(0, 0).start()
+    for part in range(2):
+        pack(near, 0, 0, part)
+        out_copy(0, 0, part).start()
     wait_group(1, 2)
     inverse(2)
-    pack(far, 1, 0)
-    out_copy(1, 0).start()
+    for part in range(2):
+        pack(far, 1, 0, part)
+        out_copy(1, 0, part).start()
     wait_group(1, 3)
     inverse(3)
-    pack(near, 0, 1)
-    out_copy(0, 1).start()
-    pack(far, 1, 1)
-    out_copy(1, 1).start()
+    for part in range(2):
+        pack(near, 0, 1, part)
+        out_copy(0, 1, part).start()
+        pack(far, 1, 1, part)
+        out_copy(1, 1, part).start()
 
     for stage in range(2):
         for pair in range(4):
             wait_group_sent(stage, pair)
     for o in range(2):
         for kind in range(2):
-            out_copy(kind, o).wait_recv()
+            for part in range(2):
+                out_copy(kind, o, part).wait_recv()
     for o in range(2):
         for kind in range(2):
-            out_copy(kind, o).wait_send()
+            for part in range(2):
+                out_copy(kind, o, part).wait_send()
 
 
 def body(orbitals):
@@ -505,8 +511,8 @@
             dma((4, GROUP)),
             dma((4, GROUP)),
             dma((4, GROUP)),
-            dma((2, 2)),
-            dma((2, 2)),
+            dma((2, 2, 2)),
+            dma((2, 2, 2)),
             dma((2, 4)),
             pltpu.SemaphoreType.REGULAR,
         ],

time: 178 us -> 178 us (level)
  no operation moved by 1% of the time
where the time goes in v4:
time: 178 us
  Pallas kernels  174 us (98%)
  other arithmetic  4.08 us (2%)
    pallas_call x1, Pallas kernels, body(): pl.pallas_call(functools.partial(kernel_body, steps, bands), out_shape=(s...  174 us
    transpose x1, other arithmetic, body(): return (near + far).transpose(1, 0, 2)  4.08 us

profile of v4, /device:TPU:33, one launch (start us, length us, event | category | flops | bytes accessed | tf_op | source)
XLA Modules:
  0.0 177.9 jit_solution(7550868738873111979)
XLA Ops:
  0.0 173.8 %shard_map.73 = (f32[15,2,14400]{2,1,0:T(2,128)}, f32[15,2,14400]{2,1,0:T(2,128)}) custom-call(f32[15,2,14400]{2,1,0:T(2,128)} %bitcast.3, bf16[128,384]{1,0:T(8,128)(2,1)} %constant.12.clone.first_ref, bf16[768,256]{1,0:T(8,128)(2,1)} %constant.13.clone.second_ref, bf16[240,720]{1,0:T(8,128)(2,1)} %constant.14.clone.third_ref, ...), custom_call_target="tpu_custom_call" | custom-call | tf_op jit(solution)/shard_map/pallas_call | solution.py:490
  173.8 4.1 %add_bitcast_fusion = f32[2,15,14400]{2,0,1:T(2,128)} fusion(f32[15,2,14400]{2,1,0:T(2,128)} %get-tuple-element.7, f32[15,2,14400]{2,1,0:T(2,128)} %get-tuple-element.8), kind=kLoop, calls=%fused_computation | loop fusion | flops 432000 | bytes 5184000 | tf_op jit(solution)/shard_map/transpose | solution.py:523
